TPU v7x, 32 devices: a whole 2x2x4 slice. The times are simulated.
32 devices in a mesh: grp: 16 (over z, y, core), mem: 2 (over x).
Axes of the slice: x: 2, y: 2, z: 4, core: 2. Of those that a mesh axis runs over, the one named last changes fastest.
Arguments:
- blocks: bfloat16 [384, 27, 128, 128], P(('grp', 'mem'))
- prolong: bfloat16 [384, 128, 128], P(('grp', 'mem'))
- cols: int32 [384, 27], P(('grp', 'mem')), may hold values from 0 to 11, as said below
- codes: int32 [384], P(('grp', 'mem')), may hold values from 1 to 15, as said below
Outputs:
- coarse_rows: bfloat16 [384, 27, 128, 128], P(('grp', 'mem'))
- diag_inverse: float32 [384, 128, 128], P('grp', 'mem')
Inputs may be any that keep to these rules, and one draw needn't show every extreme that they name: codes is the same for the fine rows in slot s of partition m of every group, and the codes of one device's 12 rows are distinct, so the matching is symmetric and a device pairs with each other group at most once. Entry 13 of every row of cols is the row's own slot.
All inputs are finite; a program needn't handle non-finite values.
Results may differ from a plain program's by a relative error of at most 0.0036.
Values may be sent and summed in bfloat16 or wider, within the bound.
A program may use at most 128 MiB of HBM per device.

v0:
```python
import jax
import jax.numpy as jnp
from jax import lax
from jax.sharding import PartitionSpec as P

NEWTON = 2


def newton_inverse(dmat):
    width = dmat.shape[1]
    eye = jnp.eye(width, dtype=jnp.float32)
    diag_vals = jnp.diagonal(dmat, axis1=1, axis2=2)
    approx = eye[None] * (1.0 / diag_vals)[:, :, None]
    for step in range(NEWTON):
        inner = jnp.einsum("sab,sbc->sac", dmat, approx, precision=lax.Precision.HIGHEST)
        approx = jnp.einsum(
            "sab,sbc->sac", approx, 2.0 * eye[None] - inner, precision=lax.Precision.HIGHEST
        )
    return approx


def local(blocks, prolong, cols, codes):
    groups = lax.axis_size("grp")
    group_index = lax.axis_index("grp")
    col_blocks = jnp.take(prolong, cols, axis=0)
    right = jnp.einsum(
        "skab,skbc->skac", blocks, col_blocks, preferred_element_type=jnp.float32
    ).astype(jnp.bfloat16)
    own_terms = jnp.einsum("sba,skbc->skac", prolong, right, preferred_element_type=jnp.float32)
    peers = group_index ^ codes
    outgoing = jnp.zeros((groups,) + right.shape[1:], jnp.bfloat16).at[peers].set(right)
    outgoing_prolong = jnp.zeros((groups,) + prolong.shape[1:], jnp.bfloat16).at[peers].set(prolong)
    arrived, arrived_prolong = (
        lax.all_to_all(outgoing, "grp", split_axis=0, concat_axis=0, tiled=True),
        lax.all_to_all(outgoing_prolong, "grp", split_axis=0, concat_axis=0, tiled=True),
    )
    partner_right = arrived[peers]
    partner_prolong = arrived_prolong[peers]
    partner_terms = jnp.einsum(
        "sba,skbc->skac", partner_prolong, partner_right, preferred_element_type=jnp.float32
    )
    total = own_terms + partner_terms
    coarse_rows = total.astype(jnp.bfloat16)
    inverse = newton_inverse(total[:, 13])
    diag_inverse = lax.all_to_all(inverse, "mem", split_axis=1, concat_axis=0, tiled=True)
    return (coarse_rows, diag_inverse)


def solution(mesh):
    in_specs = (
        P(("grp", "mem"), None, None, None),
        P(("grp", "mem"), None, None),
        P(("grp", "mem"), None),
        P(("grp", "mem")),
    )
    out_specs = (P(("grp", "mem"), None, None, None), P("grp", "mem", None))
    return jax.shard_map(local, mesh=mesh, in_specs=in_specs, out_specs=out_specs, check_vma=False)
```

profile of v0, /device:TPU:30, one launch (start us, length us, event | category | flops | bytes accessed | tf_op | source)
XLA Modules:
  0.0 495.0 jit_solution(2155788451787867182)
XLA Ops:
  2.2 2.7 scatter_fusion.1
  4.9 6.0 %all-to-all-start.1 = ((bf16[16,128,128]{2,1,0:T(8,128)(2,1)}), bf16[16,128,128]{2,1,0:T(8,128)(2,1)S(1)}, u32[]{:S(2)}, u32[]{:S(2)}) async-start(bf16[16,128,128]{2,1,0:T(8,128)(2,1)} %scatter_fusion.1), calls=%async_computation.1 | async-start | bytes 1048576 | tf_op jit(solution)/shard_map/all_to_all | solution.py:35
  12.4 11.7 %gather_fusion = bf16[324,128,128]{2,1,0:T(8,128)(2,1)} fusion(bf16[12,128,128]{2,1,0:T(8,128)(2,1)} %param.5, s32[1024]{0:T(1024)S(1)} %pad_clamp_fusion.1), kind=kCustom, calls=%fused_computation | custom fusion | bytes 21234960 | tf_op jit(solution)/shard_map/jit(_take)/gather | solution.py:25
  24.2 13.9 %copy.20 = bf16[12,27,128,128]{2,3,1,0:T(8,128)(2,1)} copy(bf16[12,27,128,128]{3,2,1,0:T(8,128)(2,1)} %bitcast.38) | data formatting | bytes 21233664 | tf_op jit(solution)/shard_map/jit(_take)/gather | solution.py:25
  38.0 14.2 %convert_bitcast_fusion = bf16[12,27,128,128]{2,3,1,0:T(8,128)(2,1)} fusion(bf16[12,27,128,128]{3,2,1,0:T(8,128)(2,1)} %param.4, bf16[12,27,128,128]{2,3,1,0:T(8,128)(2,1)} %copy.20, pred[12,27]{1,0:T(8,128)(4,1)S(1)} %compare_and_fusion), kind=kOutput, calls=%fused_computation.7 | convolution fusion | flops 1369571328 | bytes 31850820 | tf_op jit(solution)/shard_map/skab,skbc->skac/dot_general | solution.py:26
  52.2 13.9 %copy.21 = bf16[12,27,128,128]{3,2,1,0:T(8,128)(2,1)} copy(bf16[12,27,128,128]{2,3,1,0:T(8,128)(2,1)} %convert_bitcast_fusion) | data formatting | bytes 21233664 | tf_op jit(solution)/shard_map/convert_element_type | solution.py:28
  66.1 8.7 %broadcast_in_dim.35 = bf16[16,27,128,128]{3,2,1,0:T(8,128)(2,1)} broadcast(bf16[]{:T(256)} %constant.32.clone.1), dimensions={} | broadcast | bytes 14155778 | tf_op jit(solution)/shard_map/broadcast_in_dim | solution.py:31
  74.8 29.6 %scatter_fusion = bf16[16,27,128,128]{3,2,1,0:T(8,128)(2,1)} fusion(bf16[16,27,128,128]{3,2,1,0:T(8,128)(2,1)} %broadcast_in_dim.35, s32[12]{0:T(128)S(1)} %compare_select_fusion.1, bf16[12,27,128,128]{3,2,1,0:T(8,128)(2,1)} %copy.21), kind=kCustom, calls=%fused_computation.4 | custom fusion | bytes 31850544 | tf_op jit(solution)/shard_map/scatter | solution.py:31
  104.4 6.0 %all-to-all-start = ((bf16[16,27,128,128]{3,2,1,0:T(8,128)(2,1)}), bf16[16,27,128,128]{3,2,1,0:T(8,128)(2,1)}, u32[]{:S(2)}, u32[]{:S(2)}) async-start(bf16[16,27,128,128]{3,2,1,0:T(8,128)(2,1)} %scatter_fusion), calls=%async_computation | async-start | bytes 28311552 | tf_op jit(solution)/shard_map/all_to_all | solution.py:34
  111.8 303.5 %all-to-all-done = bf16[16,27,128,128]{3,2,1,0:T(8,128)(2,1)} async-done(((bf16[16,27,128,128]{3,2,1,0:T(8,128)(2,1)}), bf16[16,27,128,128]{3,2,1,0:T(8,128)(2,1)}, u32[]{:S(2)}, u32[]{:S(2)}) %all-to-all-start) | async-done | bytes 14155808 | tf_op jit(solution)/shard_map/all_to_all | solution.py:34
  415.3 11.3 %gather_fusion.1 = bf16[12,27,128,128]{3,2,1,0:T(8,128)(2,1)} fusion(bf16[16,27,128,128]{3,2,1,0:T(8,128)(2,1)} %all-to-all-done, s32[1024]{0:T(1024)S(1)} %pad_clamp_fusion), kind=kCustom, calls=%fused_computation.1 | custom fusion | bytes 21233712 | tf_op jit(solution)/shard_map/gather | solution.py:37
  426.5 12.6 %fusion.9 = f32[12,27,128,128]{3,2,1,0:T(8,128)} fusion(bf16[12,27,128,128]{3,2,1,0:T(8,128)(2,1)} %gather_fusion.1, bf16[12,128,128]{2,1,0:T(8,128)(2,1)S(1)} %gather_fusion.2), kind=kOutput, calls=%fused_computation.18 | convolution fusion | flops 1358954496 | bytes 32243712 | tf_op jit(solution)/shard_map/sba,skbc->skac/dot_general | solution.py:39
  439.2 17.2 %fusion.19 = (bf16[12,27,128,128]{2,3,1,0:T(8,128)(2,1)}, f32[12,27,128,128]{2,3,1,0:T(8,128)}) fusion(f32[12,27,128,128]{3,2,1,0:T(8,128)} %fusion.9, bf16[12,27,128,128]{2,3,1,0:T(8,128)(2,1)S(1)} %bitcast.37, bf16[12,128,128]{2,1,0:T(8,128)(2,1)S(1)} %copy-done), kind=kOutput, calls=%fused_computation.36 | convolution fusion | flops 1369571328 | bytes 64094208 | tf_op jit(solution)/shard_map/sba,skbc->skac/dot_general | solution.py:29
  456.4 1.2 slice_bitcast_fusion
  457.6 7.6 %copy.23 = f32[12,128,128]{0,2,1:T(8,128)} copy(f32[12,128,128]{1,2,0:T(8,128)S(1)} %slice_bitcast_fusion) | data formatting | bytes 1572864 | tf_op jit(solution)/shard_map/squeeze | solution.py:44
  465.3 1.9 gather_fusion.3
  467.2 2.8 convolution_subtract_fusion.1
  470.0 1.0 fusion.6
  471.0 2.6 convolution_subtract_fusion
  473.6 0.9 fusion.20
  474.5 1.4 copy.27
  475.9 4.1 all-to-all-start.2
  480.1 13.8 %copy.29 = bf16[12,27,128,128]{3,2,1,0:T(8,128)(2,1)} copy(bf16[12,27,128,128]{2,3,1,0:T(8,128)(2,1)} %get-tuple-element.8) | data formatting | bytes 21233664
  493.8 1.1 copy.28
  (26 shorter events, 4.4 us)
Async XLA Ops:
  4.9 99.5 %all-to-all-start.1 = ((bf16[16,128,128]{2,1,0:T(8,128)(2,1)}), bf16[16,128,128]{2,1,0:T(8,128)(2,1)S(1)}, u32[]{:S(2)}, u32[]{:S(2)}) async-start(bf16[16,128,128]{2,1,0:T(8,128)(2,1)} %scatter_fusion.1), calls=%async_computation.1 | async-start | bytes 1048576 | tf_op jit(solution)/shard_map/all_to_all | solution.py:35
  104.4 310.8 %all-to-all-start = ((bf16[16,27,128,128]{3,2,1,0:T(8,128)(2,1)}), bf16[16,27,128,128]{3,2,1,0:T(8,128)(2,1)}, u32[]{:S(2)}, u32[]{:S(2)}) async-start(bf16[16,27,128,128]{3,2,1,0:T(8,128)(2,1)} %scatter_fusion), calls=%async_computation | async-start | bytes 28311552 | tf_op jit(solution)/shard_map/all_to_all | solution.py:34
  415.3 23.9 %slice-start = ((s8[10616832]{0:T(1024)(128)(4,1)}), s8[2228224]{0:T(1024)(128)(4,1)S(1)}, s32[]{:S(2)}) async-start(s8[10616832]{0:T(1024)(128)(4,1)} %bitcast.36), calls=%async_computation.3 | async-start | bytes 4456448
  426.5 12.6 %copy-start = (bf16[12,128,128]{2,1,0:T(8,128)(2,1)S(1)}, bf16[12,128,128]{2,1,0:T(8,128)(2,1)}, u32[]{:S(2)}) copy-start(bf16[12,128,128]{2,1,0:T(8,128)(2,1)} %param.5) | copy-start | bytes 1179652
  426.5 12.6 %slice-start.1 = ((s8[10616832]{0:T(1024)(128)(4,1)}), s8[4194304]{0:T(1024)(128)(4,1)S(1)}, s32[]{:S(2)}) async-start(s8[10616832]{0:T(1024)(128)(4,1)} %bitcast.36), calls=%async_computation.4 | async-start | bytes 8388608
  426.5 12.6 %slice-start.2 = ((s8[10616832]{0:T(1024)(128)(4,1)}), s8[4194304]{0:T(1024)(128)(4,1)S(1)}, s32[]{:S(2)}) async-start(s8[10616832]{0:T(1024)(128)(4,1)} %bitcast.36), calls=%async_computation.5 | async-start | bytes 8388608
  456.4 10.8 %copy-start.1 = (f32[128,128]{1,0:T(8,128)S(1)}, f32[128,128]{1,0:T(8,128)}, u32[]{:S(2)}) copy-start(f32[128,128]{1,0:T(8,128)} %fusion.17) | copy-start | bytes 196612
  475.9 17.9 %all-to-all-start.2 = ((f32[12,128,128]{2,0,1:T(8,128)}), f32[12,128,128]{2,0,1:T(8,128)S(1)}, u32[]{:S(2)}, u32[]{:S(2)}) async-start(f32[12,128,128]{2,0,1:T(8,128)} %copy.27), calls=%async_computation.2 | async-start | bytes 2097152 | tf_op jit(solution)/shard_map/all_to_all | solution.py:45
where the time goes:
time: 498 us; the launch traced here: 495 us
  waiting for transfers between devices  304 us (61%)
  local copies, waits for them, and re-layouts  120 us (24%)
  matrix products  51.3 us (10%)
  starting transfers between devices  16.2 us (3%)
    all_to_all x1, waiting for transfers between devices, local(): lax.all_to_all(outgoing, 'grp', split_axis=0, concat_axis=0, tiled=True)  304 us
    scatter x1, local copies, waits for them, and re-layouts, local(): jnp.zeros((groups,) + right.shape[1:], jnp.bfloat16).at[peers].set(right)  29.6 us
    gather x2, local copies, waits for them, and re-layouts, local(): col_blocks = jnp.take(prolong, cols, axis=0)  25.6 us
    dot_general x1, matrix products, local(): jnp.einsum('sba,skbc->skac', prolong, right, preferred_element_type=jnp.f...  17.2 us
    dot_general x1, matrix products, local(): jnp.einsum('skab,skbc->skac', blocks, col_blocks, preferred_element_type=...  14.2 us
    convert_element_type x1, local copies, waits for them, and re-layouts, local(): right = jnp.einsum('skab,skbc->skac', blocks, col_blocks, preferred_eleme...  13.9 us
    unnamed x11, local copies, waits for them, and re-layouts  13.8 us
    dot_general x1, matrix products, local(): jnp.einsum('sba,skbc->skac', partner_prolong, partner_right, preferred_el...  12.6 us
  transfers between devices with their start and end apart: 3, of which 1 were waited for; matrix products, arithmetic and copies ran while one was open for 22% of the time, Pallas kernels for 0%

commit v1 on v0

v1 whole, which is shorter than its diff:
```python
import functools

import jax
import jax.numpy as jnp
from jax import lax
from jax.experimental import pallas as pl
from jax.experimental.pallas import tpu as pltpu
from jax.sharding import PartitionSpec as P

NEWTON = 2
DIAG = 13
F32 = jnp.float32
BF16 = jnp.bfloat16
MESH = pl.DeviceIdType.MESH


def xor_peer(me, code, groups):
    out = 0
    bit = 1
    while bit < groups:
        mine = (me // bit) % 2
        theirs = (code // bit) % 2
        out = out + bit * (mine + theirs - 2 * mine * theirs)
        bit *= 2
    return out


def chunk_bounds(k):
    size = -(-k // 3)
    bounds = [(a, min(size, k - a)) for a in range(0, k, size)]
    first = [c for c in bounds if c[0] <= DIAG < c[0] + c[1]]
    return first + [c for c in bounds if c not in first]


def kernel(groups, mems, chunks, blocks_hbm, prolong, cols, codes, rows_hbm, inv_hbm, *scratch):
    nq = len(chunks)
    blk, send, low, recv = (scratch[i * nq:(i + 1) * nq] for i in range(4))
    (inverse, inv_all, load_sem, store_sem, send_sem, recv_sem, msend_sem, mrecv_sem, inv_sem) = scratch[4 * nq:]
    rows, width = prolong.shape[0], prolong.shape[1]
    share = width // mems
    me = lax.axis_index("grp")
    mem = lax.axis_index("mem")

    def load(q):
        a, size = chunks[q]
        return pltpu.make_async_copy(blocks_hbm.at[:, pl.ds(a, size)], blk[q], load_sem.at[q])

    for q in range(nq):
        load(q).start()

    barrier = pltpu.get_barrier_semaphore()
    for code in range(1, groups):
        pl.semaphore_signal(
            barrier, inc=1, device_id={"grp": xor_peer(me, code, groups)}, device_id_type=MESH)
    for off in range(1, mems):
        pl.semaphore_signal(
            barrier, inc=1, device_id={"mem": lax.rem(mem + off, mems)}, device_id_type=MESH)
    pl.semaphore_wait(barrier, groups - 1 + mems - 1)

    def remote(q, code):
        return pltpu.make_async_remote_copy(
            src_ref=send[q].at[code - 1],
            dst_ref=recv[q].at[code - 1],
            send_sem=send_sem.at[q, code - 1],
            recv_sem=recv_sem.at[q, code - 1],
            device_id={"grp": xor_peer(me, code, groups)},
            device_id_type=MESH,
        )

    half = groups // 2
    for q in range(nq):
        load(q).wait()
        a, size = chunks[q]

        def one_code(i, carry, q=q, a=a, size=size):
            code = groups - 1 - i // 2 - half * (i % 2)
            slot = 0
            for s in range(rows):
                slot = slot + jnp.where(codes[s] == code, s, 0)
            left = prolong[slot].T
            for kk in range(size):
                right = jnp.dot(
                    blk[q][slot, kk], prolong[cols[slot, a + kk]], preferred_element_type=F32
                ).astype(BF16)
                term = jnp.dot(left, right, preferred_element_type=F32)
                high = term.astype(BF16)
                send[q][code - 1, kk] = high
                low[q][code - 1, kk] = (term - high.astype(F32)).astype(BF16)
            remote(q, code).start()
            return carry

        lax.fori_loop(0, groups - 1, one_code, 0)

    def pair_block(q, place, kk):
        own = send[q][place, kk].astype(F32) + low[q][place, kk].astype(F32)
        return own + recv[q][place, kk].astype(F32)

    def place_of(s):
        return jnp.maximum(codes[s] - 1, 0)

    def store(q):
        a, size = chunks[q]
        return pltpu.make_async_copy(blk[q], rows_hbm.at[:, pl.ds(a, size)], store_sem.at[q])

    def inv_remote(off):
        to = lax.rem(mem + off, mems)
        return pltpu.make_async_remote_copy(
            src_ref=inverse.at[:, pl.ds(pl.multiple_of(to * share, share), share)],
            dst_ref=inv_all.at[mem],
            send_sem=msend_sem.at[off],
            recv_sem=mrecv_sem.at[off],
            device_id={"mem": to},
            device_id_type=MESH,
        )

    for q in range(nq):
        a, size = chunks[q]

        def arrived(i, carry, q=q):
            remote(q, i + 1).wait_recv()
            return carry

        lax.fori_loop(0, groups - 1, arrived, 0)

        def one_row(s, carry, q=q, size=size):
            place = place_of(s)
            for kk in range(size):
                blk[q][s, kk] = pair_block(q, place, kk).astype(BF16)
            return carry

        lax.fori_loop(0, rows, one_row, 0)
        store(q).start()

        if a <= DIAG < a + size:
            step = max(u for u in (1, 2, 3, 4) if rows % u == 0)
            eye = (lax.broadcasted_iota(jnp.int32, (width, width), 0)
                   == lax.broadcasted_iota(jnp.int32, (width, width), 1)).astype(F32)
            dot = functools.partial(jnp.dot, precision=lax.Precision.HIGHEST, preferred_element_type=F32)

            def some_inverses(j, carry, q=q, a=a):
                mats = [pair_block(q, place_of(j * step + u), DIAG - a) for u in range(step)]
                approx = [eye * (1.0 / jnp.sum(d * eye, axis=1, keepdims=True)) for d in mats]
                for _ in range(NEWTON):
                    inner = [dot(d, x) for d, x in zip(mats, approx)]
                    approx = [dot(x, 2.0 * eye - y) for x, y in zip(approx, inner)]
                for u in range(step):
                    inverse[j * step + u] = approx[u]
                return carry

            lax.fori_loop(0, rows // step, some_inverses, 0)
            for off in range(1, mems):
                inv_remote(off).start()
            mine = pltpu.make_async_copy(
                inverse.at[:, pl.ds(pl.multiple_of(mem * share, share), share)],
                inv_all.at[mem], inv_sem.at[0])
            mine.start()
            mine.wait()

    for off in range(1, mems):
        inv_remote(off).wait()
    out = pltpu.make_async_copy(inv_all, inv_hbm, inv_sem.at[1])
    out.start()
    for q in range(nq):
        def sent(i, carry, q=q):
            remote(q, i + 1).wait_send()
            return carry

        lax.fori_loop(0, groups - 1, sent, 0)
        store(q).wait()
    out.wait()


def local(groups, mems, blocks, prolong, cols, codes):
    rows, k, width, _ = blocks.shape
    chunks = chunk_bounds(k)
    nq = len(chunks)
    share = width // mems
    peers = groups - 1
    wide = [pltpu.VMEM((peers, size, width, width), BF16) for _, size in chunks]
    scratch = (
        [pltpu.VMEM((rows, size, width, width), BF16) for _, size in chunks]
        + wide + wide + wide
        + [
            pltpu.VMEM((rows, width, width), F32),
            pltpu.VMEM((mems, rows, share, width), F32),
            pltpu.SemaphoreType.DMA((nq,)),
            pltpu.SemaphoreType.DMA((nq,)),
            pltpu.SemaphoreType.DMA((nq, peers)),
            pltpu.SemaphoreType.DMA((nq, peers)),
            pltpu.SemaphoreType.DMA((mems,)),
            pltpu.SemaphoreType.DMA((mems,)),
            pltpu.SemaphoreType.DMA((2,)),
        ]
    )
    coarse, inverse = pl.pallas_call(
        functools.partial(kernel, groups, mems, chunks),
        out_shape=(
            jax.ShapeDtypeStruct(blocks.shape, BF16),
            jax.ShapeDtypeStruct((mems, rows, share, width), F32),
        ),
        in_specs=[
            pl.BlockSpec(memory_space=pl.ANY),
            pl.BlockSpec(memory_space=pltpu.VMEM),
            pl.BlockSpec(memory_space=pltpu.SMEM),
            pl.BlockSpec(memory_space=pltpu.SMEM),
        ],
        out_specs=(pl.BlockSpec(memory_space=pl.ANY), pl.BlockSpec(memory_space=pl.ANY)),
        scratch_shapes=scratch,
        compiler_params=pltpu.CompilerParams(
            collective_id=0, has_side_effects=True, vmem_limit_bytes=60 * 1024 * 1024),
        cost_estimate=pl.CostEstimate(
            flops=4 * rows * k * width ** 3, bytes_accessed=4 * rows * k * width * width, transcendentals=0),
        name="pair_terms",
    )(blocks, prolong, cols, codes)
    return coarse, inverse.reshape(mems * rows, share, width)


def solution(mesh):
    in_specs = (
        P(("grp", "mem"), None, None, None),
        P(("grp", "mem"), None, None),
        P(("grp", "mem"), None),
        P(("grp", "mem")),
    )
    out_specs = (P(("grp", "mem"), None, None, None), P("grp", "mem", None))
    return jax.shard_map(
        functools.partial(local, mesh.shape["grp"], mesh.shape["mem"]),
        mesh=mesh, in_specs=in_specs, out_specs=out_specs, check_vma=False)
```

time: 498 us -> 338 us (0.68)
  Pallas kernels: 0 us -> 326 us
  waiting for transfers between devices: 304 us -> 0 us
  local copies, waits for them, and re-layouts: 120 us -> 10.5 us
  matrix products: 51.3 us -> 0 us
  starting transfers between devices: 16.2 us -> 0 us
    pallas_call x0 -> x1, Pallas kernels: none -> 326 us  [local(): pl.pallas_call(functools.partial(kernel, groups, mems, chunks), out_shape...]
    all_to_all x3 -> x0, waiting for transfers between devices: 304 us -> none  [the longest x1 304 us: local(): lax.all_to_all(outgoing, 'grp', split_axis=0, concat_axis=0, tiled=True)]
    dot_general x7 -> x0, matrix products: 51.3 us -> none  [the longest x1 17.2 us: local(): jnp.einsum('sba,skbc->skac', prolong, right, preferred_element_type=jnp.f...]
    gather x5 -> x0, local copies, waits for them, and re-layouts: 39.3 us -> none  [the longest x2 25.6 us: local(): col_blocks = jnp.take(prolong, cols, axis=0)]
    scatter x2 -> x0, local copies, waits for them, and re-layouts: 32.3 us -> none  [the longest x1 29.6 us: local(): jnp.zeros((groups,) + right.shape[1:], jnp.bfloat16).at[peers].set(right)]
    all_to_all x3 -> x0, starting transfers between devices: 16.2 us -> none  [the longest x1 6.02 us: local(): lax.all_to_all(outgoing, 'grp', split_axis=0, concat_axis=0, tiled=True)]
    convert_element_type x1 -> x0, local copies, waits for them, and re-layouts: 13.9 us -> none  [local(): right = jnp.einsum('skab,skbc->skac', blocks, col_blocks, preferred_eleme...]
    broadcast_in_dim x3 -> x0, local copies, waits for them, and re-layouts: 9.69 us -> none  [the longest x1 8.72 us: local(): jnp.zeros((groups,) + right.shape[1:], jnp.bfloat16).at[peers].set(right)]
  transfers between devices with their start and end apart: 3 -> 0, of which waited for: 1 -> 0; matrix products, arithmetic and copies ran while one was open for 22% -> 0% of each run, Pallas kernels for 0% -> 0%
where the time goes in v1:
time: 338 us
  Pallas kernels  326 us (96%)
  local copies, waits for them, and re-layouts  10.5 us (3%)
    pallas_call x1, Pallas kernels, local(): pl.pallas_call(functools.partial(kernel, groups, mems, chunks), out_shape...  326 us
    unnamed x4, local copies, waits for them, and re-layouts  10.5 us

profile of v1, /device:TPU:30, one launch (start us, length us, event | category | flops | bytes accessed | tf_op | source)
XLA Modules:
  0.0 337.6 jit_solution(7980198877139079811)
XLA Ops:
  0.6 326.5 %pair_terms.1 = (bf16[12,27,128,128]{3,2,1,0:T(8,128)(2,1)}, f32[2,12,64,128]{3,2,1,0:T(8,128)}) custom-call(bf16[12,27,128,128]{3,2,1,0:T(8,128)(2,1)} %blocks_hbm.1, bf16[12,128,128]{2,1,0:T(8,128)(2,1)} %prolong.1, s32[12,27]{1,0:T(8,128)} %cols.1, s32[12]{0:T(128)} %codes.1), custom_call_target="tpu_custom_call" | custom-call | flops 2717908992 | bytes 21233664 | tf_op jit(solution)/shard_map/pair_terms/pallas_call | solution.py:195
  327.1 0.0 copy-start
  327.1 9.6 %copy.8 = bf16[12,27,128,128]{3,2,1,0:T(8,128)(2,1)} copy(bf16[12,27,128,128]{3,2,1,0:T(8,128)(2,1)} %get-tuple-element.8) | data formatting | bytes 21233664
  336.7 0.0 copy-done
  336.7 0.9 copy.9
Async XLA Ops:
  327.1 9.6 %copy-start = (f32[2,12,64,128]{3,2,1,0:T(8,128)S(1)}, f32[2,12,64,128]{3,2,1,0:T(8,128)}, u32[]{:S(2)}) copy-start(f32[2,12,64,128]{3,2,1,0:T(8,128)} %get-tuple-element.5) | copy-start | bytes 2359300

commit v2 on v1

--- a/solution.py
+++ b/solution.py
@@ -12,6 +12,7 @@
 F32 = jnp.float32
 BF16 = jnp.bfloat16
 MESH = pl.DeviceIdType.MESH
+WINDOW = 2
 
 
 def xor_peer(me, code, groups):
@@ -25,11 +26,12 @@
     return out
 
 
-def chunk_bounds(k):
-    size = -(-k // 3)
-    bounds = [(a, min(size, k - a)) for a in range(0, k, size)]
-    first = [c for c in bounds if c[0] <= DIAG < c[0] + c[1]]
-    return first + [c for c in bounds if c not in first]
+def chunk_bounds(k, size=4, near=1):
+    start, end = max(DIAG - near, 0), min(DIAG + near + 1, k)
+    bounds = [(start, end - start)]
+    for low, high in ((0, start), (end, k)):
+        bounds += [(a, min(size, high - a)) for a in range(low, high, size)]
+    return bounds
 
 
 def kernel(groups, mems, chunks, blocks_hbm, prolong, cols, codes, rows_hbm, inv_hbm, *scratch):
@@ -68,11 +70,12 @@
         )
 
     half = groups // 2
-    for q in range(nq):
+
+    def send_chunk(q):
         load(q).wait()
         a, size = chunks[q]
 
-        def one_code(i, carry, q=q, a=a, size=size):
+        def one_code(i, carry):
             code = groups - 1 - i // 2 - half * (i % 2)
             slot = 0
             for s in range(rows):
@@ -86,6 +89,8 @@
                 high = term.astype(BF16)
                 send[q][code - 1, kk] = high
                 low[q][code - 1, kk] = (term - high.astype(F32)).astype(BF16)
+            if q >= WINDOW:
+                remote(q - WINDOW, code).wait_send()
             remote(q, code).start()
             return carry
 
@@ -113,59 +118,66 @@
             device_id_type=MESH,
         )
 
-    for q in range(nq):
-        a, size = chunks[q]
-
-        def arrived(i, carry, q=q):
+    def inverses(q):
+        step = max(u for u in (1, 2, 3, 4) if rows % u == 0)
+        eye = (lax.broadcasted_iota(jnp.int32, (width, width), 0)
+               == lax.broadcasted_iota(jnp.int32, (width, width), 1)).astype(F32)
+        dot = functools.partial(jnp.dot, precision=lax.Precision.HIGHEST, preferred_element_type=F32)
+
+        def some_inverses(j, carry):
+            mats = [pair_block(q, place_of(j * step + u), DIAG - chunks[q][0]) for u in range(step)]
+            approx = [eye * (1.0 / jnp.sum(d * eye, axis=1, keepdims=True)) for d in mats]
+            for _ in range(NEWTON):
+                inner = [dot(d, x) for d, x in zip(mats, approx)]
+                approx = [dot(x, 2.0 * eye - y) for x, y in zip(approx, inner)]
+            for u in range(step):
+                inverse[j * step + u] = approx[u]
+            return carry
+
+        lax.fori_loop(0, rows // step, some_inverses, 0)
+        for off in range(1, mems):
+            inv_remote(off).start()
+        mine = pltpu.make_async_copy(
+            inverse.at[:, pl.ds(pl.multiple_of(mem * share, share), share)],
+            inv_all.at[mem], inv_sem.at[0])
+        mine.start()
+        mine.wait()
+
+    def sum_chunk(q):
+        def arrived(i, carry):
             remote(q, i + 1).wait_recv()
             return carry
 
         lax.fori_loop(0, groups - 1, arrived, 0)
 
-        def one_row(s, carry, q=q, size=size):
+        def one_row(s, carry):
             place = place_of(s)
-            for kk in range(size):
+            for kk in range(chunks[q][1]):
                 blk[q][s, kk] = pair_block(q, place, kk).astype(BF16)
             return carry
 
         lax.fori_loop(0, rows, one_row, 0)
         store(q).start()
-
-        if a <= DIAG < a + size:
-            step = max(u for u in (1, 2, 3, 4) if rows % u == 0)
-            eye = (lax.broadcasted_iota(jnp.int32, (width, width), 0)
-                   == lax.broadcasted_iota(jnp.int32, (width, width), 1)).astype(F32)
-            dot = functools.partial(jnp.dot, precision=lax.Precision.HIGHEST, preferred_element_type=F32)
-
-            def some_inverses(j, carry, q=q, a=a):
-                mats = [pair_block(q, place_of(j * step + u), DIAG - a) for u in range(step)]
-                approx = [eye * (1.0 / jnp.sum(d * eye, axis=1, keepdims=True)) for d in mats]
-                for _ in range(NEWTON):
-                    inner = [dot(d, x) for d, x in zip(mats, approx)]
-                    approx = [dot(x, 2.0 * eye - y) for x, y in zip(approx, inner)]
-                for u in range(step):
-                    inverse[j * step + u] = approx[u]
-                return carry
-
-            lax.fori_loop(0, rows // step, some_inverses, 0)
-            for off in range(1, mems):
-                inv_remote(off).start()
-            mine = pltpu.make_async_copy(
-                inverse.at[:, pl.ds(pl.multiple_of(mem * share, share), share)],
-                inv_all.at[mem], inv_sem.at[0])
-            mine.start()
-            mine.wait()
+        if chunks[q][0] <= DIAG < chunks[q][0] + chunks[q][1]:
+            inverses(q)
+
+    for q in range(nq + WINDOW):
+        if q < nq:
+            send_chunk(q)
+        if q >= WINDOW:
+            sum_chunk(q - WINDOW)
 
     for off in range(1, mems):
         inv_remote(off).wait()
     out = pltpu.make_async_copy(inv_all, inv_hbm, inv_sem.at[1])
     out.start()
-    for q in range(nq):
+    for q in range(max(nq - WINDOW, 0), nq):
         def sent(i, carry, q=q):
             remote(q, i + 1).wait_send()
             return carry
 
         lax.fori_loop(0, groups - 1, sent, 0)
+    for q in range(nq):
         store(q).wait()
     out.wait()
 

time: 338 us -> 328 us (0.970)
  Pallas kernels: 326 us -> 313 us
    pallas_call x1, Pallas kernels: 326 us -> 313 us  [local(): pl.pallas_call(functools.partial(kernel, groups, mems, chunks), out_shape...]
where the time goes in v2:
time: 328 us; the launch traced here: 324 us
  Pallas kernels  313 us (95%)
  local copies, waits for them, and re-layouts  10.5 us (3%)
    pallas_call x1, Pallas kernels, local(): pl.pallas_call(functools.partial(kernel, groups, mems, chunks), out_shape...  313 us
    unnamed x4, local copies, waits for them, and re-layouts  10.5 us

profile of v2, /device:TPU:30, one launch (start us, length us, event | category | flops | bytes accessed | tf_op | source)
XLA Modules:
  0.0 324.3 jit_solution(14451802634769105914)
XLA Ops:
  0.6 313.2 %pair_terms.1 = (bf16[12,27,128,128]{3,2,1,0:T(8,128)(2,1)}, f32[2,12,64,128]{3,2,1,0:T(8,128)}) custom-call(bf16[12,27,128,128]{3,2,1,0:T(8,128)(2,1)} %blocks_hbm.1, bf16[12,128,128]{2,1,0:T(8,128)(2,1)} %prolong.1, s32[12,27]{1,0:T(8,128)} %cols.1, s32[12]{0:T(128)} %codes.1), custom_call_target="tpu_custom_call" | custom-call | flops 2717908992 | bytes 21233664 | tf_op jit(solution)/shard_map/pair_terms/pallas_call | solution.py:207
  313.8 0.0 copy-start
  313.8 9.6 %copy.8 = bf16[12,27,128,128]{3,2,1,0:T(8,128)(2,1)} copy(bf16[12,27,128,128]{3,2,1,0:T(8,128)(2,1)} %get-tuple-element.8) | data formatting | bytes 21233664
  323.4 0.0 copy-done
  323.4 0.9 copy.9
Async XLA Ops:
  313.8 9.6 %copy-start = (f32[2,12,64,128]{3,2,1,0:T(8,128)S(1)}, f32[2,12,64,128]{3,2,1,0:T(8,128)}, u32[]{:S(2)}) copy-start(f32[2,12,64,128]{3,2,1,0:T(8,128)} %get-tuple-element.5) | copy-start | bytes 2359300

commit v3 on v2

--- a/solution.py
+++ b/solution.py
@@ -13,6 +13,7 @@
 BF16 = jnp.bfloat16
 MESH = pl.DeviceIdType.MESH
 WINDOW = 2
+MAX_DROP = 2
 
 
 def xor_peer(me, code, groups):
@@ -26,18 +27,23 @@
     return out
 
 
-def chunk_bounds(k, size=4, near=1):
-    start, end = max(DIAG - near, 0), min(DIAG + near + 1, k)
-    bounds = [(start, end - start)]
+def chunk_bounds(k, size=4):
+    start, end = max(DIAG - 1, 0), min(DIAG + 2, k)
+    bounds = [(DIAG, 1)] + [(a, 1) for a in range(start, end) if a != DIAG]
     for low, high in ((0, start), (end, k)):
         bounds += [(a, min(size, high - a)) for a in range(low, high, size)]
     return bounds
 
 
-def kernel(groups, mems, chunks, blocks_hbm, prolong, cols, codes, rows_hbm, inv_hbm, *scratch):
+def kernel(groups, mems, chunks, drop, blocks_hbm, prolong, cols, codes, rows_hbm, inv_hbm, *scratch):
     nq = len(chunks)
     blk, send, low, recv = (scratch[i * nq:(i + 1) * nq] for i in range(4))
-    (inverse, inv_all, load_sem, store_sem, send_sem, recv_sem, msend_sem, mrecv_sem, inv_sem) = scratch[4 * nq:]
+    hop = scratch[4 * nq:5 * nq] if drop else None
+    (inverse, inv_all, load_sem, store_sem, send_sem, recv_sem, msend_sem, mrecv_sem, inv_sem,
+     *hop_sems) = scratch[(5 if drop else 4) * nq:]
+    half = groups // 2
+    kept = groups - 1 - drop
+    stages = (groups - 1).bit_length() - 1
     rows, width = prolong.shape[0], prolong.shape[1]
     share = width // mems
     me = lax.axis_index("grp")
@@ -69,39 +75,115 @@
             device_id_type=MESH,
         )
 
-    half = groups // 2
+    dropped = [groups - 1 - i for i in range(drop)]
+    riding = [jnp.int32(0)] * drop
+    if drop:
+        taken = {}
+        for c in range(half, groups):
+            taken[c] = sum(jnp.where(codes[s] == c, 1, 0) for s in range(rows))
+        rank, count = [], jnp.int32(0)
+        for c in dropped:
+            rank.append(count)
+            count = count + taken[c]
+        free = jnp.int32(0)
+        for c in range(half, kept + 1):
+            for i, d in enumerate(dropped):
+                fits = jnp.logical_and(
+                    jnp.logical_and(taken[c] == 0, taken[d] == 1), free == rank[i])
+                riding[i] = jnp.where(fits, c, riding[i])
+            free = free + (1 - taken[c])
+
+    def slot_of(code):
+        slot = 0
+        for s in range(rows):
+            slot = slot + jnp.where(codes[s] == code, s, 0)
+        return slot
+
+    def make_terms(q, code):
+        a, size = chunks[q]
+        slot = slot_of(code)
+        left = prolong[slot].T
+        for kk in range(size):
+            right = jnp.dot(
+                blk[q][slot, kk], prolong[cols[slot, a + kk]], preferred_element_type=F32
+            ).astype(BF16)
+            term = jnp.dot(left, right, preferred_element_type=F32)
+            high = term.astype(BF16)
+            low[q][code - 1, kk] = (term - high.astype(F32)).astype(BF16)
+            if drop and not isinstance(code, int):
+                for i in range(drop):
+                    high = jnp.where(code == riding[i], hop[q][stages - 2, i, kk], high)
+            send[q][code - 1, kk] = high
+
+    def held(q, stage, i):
+        if stage == 0:
+            return send[q].at[dropped[i] - 1]
+        if stage == 1:
+            return recv[q].at[dropped[i] - 1]
+        return hop[q].at[stage - 2, i]
+
+    def exchange(q, stage, i):
+        return pltpu.make_async_remote_copy(
+            src_ref=held(q, stage, i),
+            dst_ref=held(q, stage + 1, i),
+            send_sem=hop_sems[0].at[q, stage, i],
+            recv_sem=hop_sems[1].at[q, stage, i],
+            device_id={"grp": xor_peer(me, 2 ** stage, groups)},
+            device_id_type=MESH,
+        )
+
+    def hops_at(time):
+        if not drop:
+            return []
+        return [(time + stages - b, b) for b in range(stages) if 0 <= time + stages - b < nq]
+
+    def start_hops(time):
+        for q, b in reversed(hops_at(time)):
+            if b == 0:
+                load(q).wait()
+                for code in dropped:
+                    make_terms(q, code)
+            for i in range(drop):
+                exchange(q, b, i).start()
+
+    def finish_hops(time):
+        for q, b in reversed(hops_at(time)):
+            for i in range(drop):
+                exchange(q, b, i).wait()
+                ride = jnp.where(riding[i] == 0, dropped[i], riding[i])
+                moves = (ride // 2 ** b) % 2 != (dropped[i] // 2 ** b) % 2
+                before, after = held(q, b, i), held(q, b + 1, i)
+                for kk in range(chunks[q][1]):
+                    after[kk] = jnp.where(moves, after[kk], before[kk])
 
     def send_chunk(q):
-        load(q).wait()
-        a, size = chunks[q]
+        if not drop:
+            load(q).wait()
 
         def one_code(i, carry):
-            code = groups - 1 - i // 2 - half * (i % 2)
-            slot = 0
-            for s in range(rows):
-                slot = slot + jnp.where(codes[s] == code, s, 0)
-            left = prolong[slot].T
-            for kk in range(size):
-                right = jnp.dot(
-                    blk[q][slot, kk], prolong[cols[slot, a + kk]], preferred_element_type=F32
-                ).astype(BF16)
-                term = jnp.dot(left, right, preferred_element_type=F32)
-                high = term.astype(BF16)
-                send[q][code - 1, kk] = high
-                low[q][code - 1, kk] = (term - high.astype(F32)).astype(BF16)
+            if half - drop >= half - 1:
+                code = kept - i // 2 - (half - drop) * (i % 2)
+            else:
+                code = half - 1 - i // 2 + (half - drop) * (i % 2)
+            make_terms(q, code)
             if q >= WINDOW:
                 remote(q - WINDOW, code).wait_send()
             remote(q, code).start()
             return carry
 
-        lax.fori_loop(0, groups - 1, one_code, 0)
+        lax.fori_loop(0, kept, one_code, 0)
 
     def pair_block(q, place, kk):
-        own = send[q][place, kk].astype(F32) + low[q][place, kk].astype(F32)
-        return own + recv[q][place, kk].astype(F32)
+        mine, theirs = place
+        own = send[q][mine, kk].astype(F32) + low[q][mine, kk].astype(F32)
+        return own + recv[q][theirs, kk].astype(F32)
 
     def place_of(s):
-        return jnp.maximum(codes[s] - 1, 0)
+        mine = codes[s]
+        theirs = mine
+        for i in range(drop):
+            theirs = jnp.where(mine == dropped[i], riding[i], theirs)
+        return jnp.maximum(mine - 1, 0), jnp.maximum(theirs - 1, 0)
 
     def store(q):
         a, size = chunks[q]
@@ -148,7 +230,7 @@
             remote(q, i + 1).wait_recv()
             return carry
 
-        lax.fori_loop(0, groups - 1, arrived, 0)
+        lax.fori_loop(0, kept, arrived, 0)
 
         def one_row(s, carry):
             place = place_of(s)
@@ -161,11 +243,17 @@
         if chunks[q][0] <= DIAG < chunks[q][0] + chunks[q][1]:
             inverses(q)
 
+    for time in range(-stages, 0):
+        start_hops(time)
+        finish_hops(time)
     for q in range(nq + WINDOW):
         if q < nq:
+            start_hops(q)
             send_chunk(q)
         if q >= WINDOW:
             sum_chunk(q - WINDOW)
+        if q < nq:
+            finish_hops(q)
 
     for off in range(1, mems):
         inv_remote(off).wait()
@@ -176,22 +264,24 @@
             remote(q, i + 1).wait_send()
             return carry
 
-        lax.fori_loop(0, groups - 1, sent, 0)
+        lax.fori_loop(0, kept, sent, 0)
     for q in range(nq):
         store(q).wait()
     out.wait()
 
 
-def local(groups, mems, blocks, prolong, cols, codes):
+def pair_terms(groups, mems, drop, blocks, prolong, cols, codes):
     rows, k, width, _ = blocks.shape
     chunks = chunk_bounds(k)
     nq = len(chunks)
     share = width // mems
     peers = groups - 1
+    stages = peers.bit_length() - 1
     wide = [pltpu.VMEM((peers, size, width, width), BF16) for _, size in chunks]
     scratch = (
         [pltpu.VMEM((rows, size, width, width), BF16) for _, size in chunks]
         + wide + wide + wide
+        + ([pltpu.VMEM((stages - 1, drop, size, width, width), BF16) for _, size in chunks] if drop else [])
         + [
             pltpu.VMEM((rows, width, width), F32),
             pltpu.VMEM((mems, rows, share, width), F32),
@@ -203,9 +293,10 @@
             pltpu.SemaphoreType.DMA((mems,)),
             pltpu.SemaphoreType.DMA((2,)),
         ]
+        + ([pltpu.SemaphoreType.DMA((nq, stages, drop))] * 2 if drop else [])
     )
     coarse, inverse = pl.pallas_call(
-        functools.partial(kernel, groups, mems, chunks),
+        functools.partial(kernel, groups, mems, chunks, drop),
         out_shape=(
             jax.ShapeDtypeStruct(blocks.shape, BF16),
             jax.ShapeDtypeStruct((mems, rows, share, width), F32),
@@ -219,12 +310,20 @@
         out_specs=(pl.BlockSpec(memory_space=pl.ANY), pl.BlockSpec(memory_space=pl.ANY)),
         scratch_shapes=scratch,
         compiler_params=pltpu.CompilerParams(
-            collective_id=0, has_side_effects=True, vmem_limit_bytes=60 * 1024 * 1024),
+            collective_id=drop, has_side_effects=True, vmem_limit_bytes=62 * 1024 * 1024),
         cost_estimate=pl.CostEstimate(
             flops=4 * rows * k * width ** 3, bytes_accessed=4 * rows * k * width * width, transcendentals=0),
-        name="pair_terms",
+        name="pair_terms_%d" % drop,
     )(blocks, prolong, cols, codes)
     return coarse, inverse.reshape(mems * rows, share, width)
+
+
+def local(groups, mems, blocks, prolong, cols, codes):
+    half = groups // 2
+    absent = half - jnp.sum((codes >= half).astype(jnp.int32))
+    drop = jnp.clip(lax.pmin(absent, "mem"), 0, MAX_DROP)
+    branches = [functools.partial(pair_terms, groups, mems, d) for d in range(MAX_DROP + 1)]
+    return lax.switch(drop, branches, blocks, prolong, cols, codes)
 
 
 def solution(mesh):

time: 328 us -> 305 us (0.930)
  Pallas kernels: 313 us -> 283 us
  blocking collectives: 0 us -> 4.8 us
    pallas_call x1, Pallas kernels: 313 us -> 283 us  [pair_terms(): pl.pallas_call(functools.partial(kernel, groups, mems, chunks, drop), out...]
    pmin x0 -> x1, blocking collectives: none -> 4.8 us  [local(): drop = jnp.clip(lax.pmin(absent, 'mem'), 0, MAX_DROP)]
    unnamed x4 -> x2, local copies, waits for them, and re-layouts: 10.5 us -> 10.4 us
where the time goes in v3:
time: 305 us; the launch traced here: 302 us
  Pallas kernels  283 us (93%)
  local copies, waits for them, and re-layouts  10.4 us (3%)
  blocking collectives  4.8 us (2%)
    pallas_call x1, Pallas kernels, pair_terms(): pl.pallas_call(functools.partial(kernel, groups, mems, chunks, drop), out...  283 us
    unnamed x2, local copies, waits for them, and re-layouts  10.4 us

profile of v3, /device:TPU:30, one launch (start us, length us, event | category | flops | bytes accessed | tf_op | source)
XLA Modules:
  0.0 302.1 jit_solution(18312989970401543235)
XLA Ops:
  0.6 1.3 fusion
  2.6 4.8 %pmin.7 = s32[]{:T(128)} all-reduce(s32[]{:T(128)S(6)} %sub.3), channel_id=1, replica_groups=mesh['grp'=16,'mem'=2] {'mem'}, use_global_device_ids=true, to_apply=%region_1.0 | all-reduce | flops 1 | bytes 8 | tf_op jit(solution)/shard_map/pmin | solution.py:324
  8.0 283.6 %conditional.1 = (bf16[12,27,128,128]{3,2,1,0:T(8,128)(2,1)}, f32[24,64,128]{2,1,0:T(8,128)S(1)}) conditional(s32[]{:T(128)} %clamp.3, (bf16[12,27,128,128]{3,2,1,0:T(8,128)(2,1)}, bf16[12,128,128]{2,1,0:T(8,128)(2,1)}, s32[12,27]{1,0:T(8,128)}, s32[12]{0:T(128)}) %tuple.19, (bf16[12,27,128,128]{3,2,1,0:T(8,128)(2,1)}, ...), branch_computations={%region_2.3_spmd, %region_3.4_spmd, %region_4.5_spmd} | conditional | flops 2717908992 | bytes 21233680 | solution.py:326
  8.1 283.2 %pair_terms_1.1 = (bf16[12,27,128,128]{3,2,1,0:T(8,128)(2,1)}, f32[2,12,64,128]{3,2,1,0:T(8,128)S(1)}) custom-call(bf16[12,27,128,128]{3,2,1,0:T(8,128)(2,1)} %get-tuple-element.55.blocks_hbm, bf16[12,128,128]{2,1,0:T(8,128)(2,1)} %get-tuple-element.58.prolong, s32[12,27]{1,0:T(8,128)} %get-tuple-element.61.cols, s32[12]{0:T(128)} %get-tuple-element.33.codes), custom_call_target="tpu_custom_call" | custom-call | flops 2717908992 | bytes 21233664 | tf_op jit(solution)/shard_map/cond/branch_1_fun/pair_terms_1/pallas_call | solution.py:298
  291.7 9.5 %copy.26 = bf16[12,27,128,128]{3,2,1,0:T(8,128)(2,1)} copy(bf16[12,27,128,128]{3,2,1,0:T(8,128)(2,1)} %get-tuple-element.71) | data formatting | bytes 21233664
  301.2 0.9 copy.27
